TPU v7x, 32 devices: a whole 2x2x4 slice. The times are simulated.
32 devices in a mesh: depth: 4 (over z), freq: 8 (over y, x, core).
Axes of the slice: x: 2, y: 2, z: 4, core: 2. Of those that a mesh axis runs over, the one named last changes fastest.
Arguments:
- source: float32 [8, 2, 256, 256], P('freq'), may hold values from -6 to 6
- receiver: float32 [8, 2, 256, 256], P('freq'), may hold values from -6 to 6
- classes: int32 [4, 256, 256], P('depth'), may hold values from 0 to 15
- coef_table: float32 [16, 8, 2, 6], replicated, may hold values from -2 to 2, as said below
- freq_list: int32 [8], P('freq'), may hold values from 0 to 7, each once
Outputs:
- image: float32 [256, 4, 8, 256], P('freq', 'depth')
Inputs may be any that keep to these rules, and one draw needn't show every extreme that they name: `coef_table`: every entry lies within the stated bounds.
All inputs are finite; a program needn't handle non-finite values.
Results may differ from a plain program's by a relative error of at most 0.00011.
Values sent between devices are 32-bit elements; how exact they have to be, the bound alone decides.
A program may use at most 64 MiB of HBM per device.

v0:
```python
import functools

import jax
import jax.numpy as jnp
from jax import lax
from jax.experimental import pallas as pl
from jax.experimental.pallas import tpu as pltpu
from jax.sharding import PartitionSpec as P

H = 8
LANES = 128
SUB = 8


def flip_rows(v, sub):
    v = pltpu.roll(v, 4, 0)
    v = jnp.where((sub & 2) == 0, pltpu.roll(v, 6, 0), pltpu.roll(v, 2, 0))
    return jnp.where((sub & 1) == 0, pltpu.roll(v, 7, 0), pltpu.roll(v, 1, 0))


def kernel(
    cfg,
    source,
    receiver,
    classes,
    coef,
    freq_row,
    out,
    tables,
    fields,
    mirrored,
    cls,
    terms,
    pair_buf,
    ring_buf,
    done_buf,
    load_sem,
    own_cls_sem,
    cls_send,
    cls_recv,
    fwd_send,
    fwd_recv,
    pair_send,
    pair_recv,
    ring_send,
    ring_recv,
    out_send,
    out_recv,
    *higher,
):
    nd, nf, rows_x, cols_y, K, W = (cfg[n] for n in ("nd", "nf", "rows_x", "cols_y", "K", "W"))
    nh = cols_y // LANES
    rows_here = rows_x // nd
    half = rows_here // 2
    groups = nf // 2
    piece = rows_here // nf
    rows_out = rows_x // nf
    owners = nf // nd
    out_parts = rows_out // piece
    wide = (W - rows_here) // 2
    cls_half = W // 2

    d = lax.axis_index("depth")
    f = lax.axis_index("freq")
    core = lax.rem(f, 2)
    chip = f // 2
    mate = f + 1 - 2 * core

    def window(depth):
        return pl.multiple_of(jnp.minimum(jnp.maximum(depth * rows_here - wide, 0), rows_x - W), SUB)

    start = window(d)
    base = pl.multiple_of(d * rows_here - start, SUB)

    def remote(src, dst, send, recv, dep, fre):
        return pltpu.make_async_remote_copy(
            src_ref=src,
            dst_ref=dst,
            send_sem=send,
            recv_sem=recv,
            device_id={"depth": dep, "freq": fre},
            device_id_type=pl.DeviceIdType.MESH,
        )

    place = core * half + chip * piece
    goal = d * owners + place // rows_out
    goal_part = lax.rem(place, rows_out) // piece
    from_depth = f // owners

    def giver(part):
        row = lax.rem(f, owners) * rows_out + part * piece
        return 2 * (lax.rem(row, half) // piece) + row // half

    def is_mine(part):
        return jnp.logical_and(from_depth == d, giver(part) == f)

    loads = []
    for comp in range(4):
        ref = source if comp < 2 else receiver
        for h in range(nh):
            loads.append(
                pltpu.make_async_copy(
                    ref.at[0, comp % 2, pl.ds(start, W), pl.ds(h * LANES, LANES)],
                    fields.at[comp, h, pl.ds(SUB, W), :],
                    load_sem.at[comp * nh + h],
                )
            )
            loads[-1].start()
    own_cls = pltpu.make_async_copy(classes.at[0, pl.ds(start, W)], cls.at[d], own_cls_sem)
    own_cls.start()

    barrier = pltpu.get_barrier_semaphore()

    def greet(dep, fre):
        pl.semaphore_signal(
            barrier,
            inc=1,
            device_id={"depth": dep, "freq": fre},
            device_id_type=pl.DeviceIdType.MESH,
        )

    for s in range(1, nd):
        greet(lax.rem(d + s, nd), f)
    greet(d, mate)
    for s in range(1, groups):
        greet(d, 2 * lax.rem(chip + s, groups) + core)
    for part in range(out_parts):

        @pl.when(jnp.logical_not(is_mine(part)))
        def _():
            greet(from_depth, giver(part))

    targets = (nd - 1) + 1 + (groups - 1) + nd
    pl.semaphore_wait(barrier, targets - jnp.where(goal == f, 1, 0))

    cls_rows = pl.multiple_of(core * cls_half, SUB)
    cls_copies = []
    for s in range(1, nd):
        to = lax.rem(d + s, nd)
        src_row = pl.multiple_of(window(to) + cls_rows, SUB)
        copy = remote(
            classes.at[0, pl.ds(src_row, cls_half)],
            cls.at[d, pl.ds(cls_rows, cls_half)],
            cls_send.at[s - 1],
            cls_recv.at[d],
            to,
            f,
        )
        copy.start()
        cls_copies.append(copy)

    def forward(l):
        part = cls.at[l, pl.ds(cls_rows, cls_half)]
        return remote(part, part, fwd_send.at[l], fwd_recv.at[l], d, mate)

    def pass_on(l):
        @pl.when(d != l)
        def _():
            part = cls.at[l, pl.ds(cls_rows, cls_half)]
            remote(part, part, cls_send.at[0], cls_recv.at[l], d, mate).wait_recv()
            forward(l).start()

    def classes_ready(l):
        @pl.when(d != l)
        def _():
            forward(l).wait_recv()

        @pl.when(d == l)
        def _():
            own_cls.wait()

    held = (fields,) + higher
    row = freq_row[0]
    for k in range(K):
        for p in range(2):
            at = p * K + k
            tables[at : at + 1, 0 : coef.shape[3]] = coef[row, k, p : p + 1, :]
    zero = jnp.zeros((SUB, LANES), jnp.float32)
    for comp in range(4):
        for h in range(nh):
            for ref in held:
                ref[comp, h, 0:SUB, :] = zero
                ref[comp, h, W + SUB : W + 2 * SUB, :] = zero
            if comp < 2:
                mirrored[comp, h, 0:SUB, :] = zero
                mirrored[comp, h, W + SUB : W + 2 * SUB, :] = zero

    lane = lax.broadcasted_iota(jnp.int32, (SUB, LANES), 1)
    sub = lax.broadcasted_iota(jnp.int32, (SUB, LANES), 0)
    first_lane = lane == 0
    last_lane = lane == LANES - 1

    for copy in loads:
        copy.wait()

    def chebyshev(k):
        for r0 in range(0, W, SUB):
            for comp in range(4):
                twice, single, along, lefts, rights = [], [], [], [], []
                for h in range(nh):
                    v = held[k - 1][comp, h, pl.ds(r0 + SUB, SUB), :]
                    up = held[k - 1][comp, h, pl.ds(r0 + SUB - 1, SUB), :]
                    down = held[k - 1][comp, h, pl.ds(r0 + SUB + 1, SUB), :]
                    v2 = v + v
                    x_sum = up + down + v2
                    single.append(v)
                    twice.append(v2)
                    along.append(x_sum)
                    lefts.append(pltpu.roll(x_sum, 1, 1))
                    rights.append(pltpu.roll(x_sum, LANES - 1, 1))
                for h in range(nh):
                    left = jnp.where(first_lane, lefts[h - 1] if h > 0 else 0.0, lefts[h])
                    right = jnp.where(last_lane, rights[h + 1] if h + 1 < nh else 0.0, rights[h])
                    total = left + right + (along[h] + along[h])
                    if k == 1:
                        result = 0.125 * total - single[h]
                    else:
                        earlier = held[k - 2][comp, h, pl.ds(r0 + SUB, SUB), :]
                        result = 0.25 * total - (twice[h] + earlier)
                    held[k][comp, h, pl.ds(r0 + SUB, SUB), :] = result

    def combine(l):
        for r0 in range(0, W, SUB):
            rows = pl.ds(r0 + SUB, SUB)
            for h in range(nh):
                which = cls[l, pl.ds(r0, SUB), h * LANES : (h + 1) * LANES]
                sums = None
                for k in range(K):
                    cr, ci = (
                        jnp.take_along_axis(
                            jnp.broadcast_to(tables[p * K + k : p * K + k + 1, :], (SUB, LANES)),
                            which,
                            axis=1,
                            mode="promise_in_bounds",
                        )
                        for p in range(2)
                    )
                    sr, si, rr, ri = (held[k][comp, h, rows, :] for comp in range(4))
                    new = (
                        cr * sr + ci * si,
                        cr * si - ci * sr,
                        cr * rr - ci * ri,
                        cr * ri + ci * rr,
                    )
                    sums = new if sums is None else tuple(a + b for a, b in zip(sums, new))
                for comp in range(4):
                    fields[comp, h, rows, :] = sums[comp]
                for comp in range(2):
                    mirrored[comp, h, pl.ds(W - r0, SUB), :] = flip_rows(
                        sums[comp], sub
                    )

    def correlate(l, first):
        group = min(16, half)

        def step(i, carry):
            for g in range(group):
                r = first + i * group + g
                x = base + r
                for h in range(nh):
                    total = None
                    for part in range(2):
                        src = mirrored[part, h, pl.ds(W + 3 - x, SUB), :]
                        rec = fields[2 + part, h, pl.ds(x + 4, SUB), :]
                        total = src * rec if total is None else total + src * rec
                    terms[l, r, :, h * LANES : (h + 1) * LANES] = total
            return carry

        lax.fori_loop(0, half // group, step, 0)

    def pair_copy(l):
        return remote(
            terms.at[l, pl.ds((1 - core) * half, half)],
            pair_buf.at[l],
            pair_send.at[l],
            pair_recv.at[l],
            d,
            mate,
        )

    def ring_copy(l, s):
        other = lax.rem(chip + s, groups)
        return remote(
            terms.at[l, pl.ds(core * half + other * piece, piece)],
            ring_buf.at[l, s - 1],
            ring_send.at[l, s - 1],
            ring_recv.at[l, s - 1],
            d,
            2 * other + core,
        )

    def out_copy(l):
        return remote(
            done_buf.at[l],
            out.at[pl.ds(goal_part * piece, piece), 0],
            out_send.at[l],
            out_recv.at[goal_part],
            l,
            goal,
        )

    def pair_sum(l):
        pair_copy(l).wait_recv()
        for s in list(range(1, groups)) + [0]:
            at = lax.rem(chip + s, groups) * piece
            rows = pl.ds(core * half + at, piece)
            terms[l, rows] = terms[l, rows] + pair_buf[l, pl.ds(at, piece)]
            if s > 0:
                ring_copy(l, s).start()

    def ring_sum(l):
        total = terms[l, pl.ds(place, piece)]
        for s in range(1, groups):
            ring_copy(l, s).wait_recv()
            total = total + ring_buf[l, s - 1]
        mine = jnp.logical_and(l == d, goal == f)

        @pl.when(mine)
        def _():
            out[pl.ds(goal_part * piece, piece), 0] = total

        @pl.when(jnp.logical_not(mine))
        def _():
            done_buf[l] = total
            out_copy(l).start()

    def level(l, carry):
        for k in range(1, K):
            chebyshev(k)

        @pl.when(l == 0)
        def _():
            pass_on(0)

        @pl.when(l > 0)
        def _():
            pair_sum(l - 1)

        classes_ready(l)
        combine(l)
        correlate(l, (1 - core) * half)
        pair_copy(l).start()
        correlate(l, core * half)

        @pl.when(l + 1 < nd)
        def _():
            pass_on(l + 1)

        @pl.when(l > 1)
        def _():
            ring_sum(l - 2)

        return carry

    lax.fori_loop(0, nd, level, 0)
    if nd >= 2:
        ring_sum(nd - 2)
    pair_sum(nd - 1)
    ring_sum(nd - 1)

    for copy in cls_copies:
        copy.wait_send()
    for l in range(nd):

        @pl.when(d != l)
        def _():
            forward(l).wait_send()

        pair_copy(l).wait_send()
        for s in range(1, groups):
            ring_copy(l, s).wait_send()

        @pl.when(jnp.logical_not(jnp.logical_and(l == d, goal == f)))
        def _():
            out_copy(l).wait_send()

    for part in range(out_parts):

        @pl.when(jnp.logical_not(is_mine(part)))
        def _():
            remote(
                done_buf.at[0],
                out.at[pl.ds(part * piece, piece), 0],
                out_send.at[0],
                out_recv.at[part],
                from_depth,
                giver(part),
            ).wait_recv()


def solution(mesh):
    nd, nf = mesh.shape["depth"], mesh.shape["freq"]

    def per_device(source, receiver, classes, coef_table, freq_list):
        rows_x, cols_y = source.shape[2], source.shape[3]
        K = coef_table.shape[3]
        rows_here = rows_x // nd
        reach = nd * (K - 1) + H // 2
        wide = -(-reach // SUB) * SUB
        W = min(rows_x, rows_here + 2 * wide)
        nh = cols_y // LANES
        groups = nf // 2
        piece = rows_here // nf
        rows_out = rows_x // nf
        cfg = dict(nd=nd, nf=nf, rows_x=rows_x, cols_y=cols_y, K=K, W=W)
        coef = jnp.transpose(coef_table, (1, 3, 2, 0))
        hbm = pl.BlockSpec(memory_space=pltpu.HBM)
        vmem = pl.BlockSpec(memory_space=pltpu.VMEM)
        dma = pltpu.SemaphoreType.DMA
        field = pltpu.VMEM((4, nh, W + 2 * SUB, LANES), jnp.float32)
        summed = pl.pallas_call(
            functools.partial(kernel, cfg),
            out_shape=jax.ShapeDtypeStruct((rows_out, 1, H, cols_y), jnp.float32),
            in_specs=[hbm, hbm, hbm, vmem, pl.BlockSpec(memory_space=pltpu.SMEM)],
            out_specs=vmem,
            scratch_shapes=[
                pltpu.VMEM((2 * K, LANES), jnp.float32),
                field,
                pltpu.VMEM((2, nh, W + 2 * SUB, LANES), jnp.float32),
                pltpu.VMEM((nd, W, cols_y), jnp.int32),
                pltpu.VMEM((nd, rows_here, H, cols_y), jnp.float32),
                pltpu.VMEM((nd, rows_here // 2, H, cols_y), jnp.float32),
                pltpu.VMEM((nd, max(groups - 1, 1), piece, H, cols_y), jnp.float32),
                pltpu.VMEM((nd, piece, H, cols_y), jnp.float32),
                dma((4 * nh,)),
                dma,
                dma((nd,)),
                dma((nd,)),
                dma((nd,)),
                dma((nd,)),
                dma((nd,)),
                dma((nd,)),
                dma((nd, max(groups - 1, 1))),
                dma((nd, max(groups - 1, 1))),
                dma((nd,)),
                dma((rows_out // piece,)),
            ]
            + [field] * (K - 1),
            compiler_params=pltpu.CompilerParams(
                collective_id=0, has_side_effects=True, vmem_limit_bytes=62 * 1024 * 1024
            ),
        )(source, receiver, classes, coef, freq_list)
        return summed * float(nf) ** -0.5

    return jax.shard_map(
        per_device,
        mesh=mesh,
        in_specs=(
            P("freq", None, None, None),
            P("freq", None, None, None),
            P("depth", None, None),
            P(),
            P("freq"),
        ),
        out_specs=P("freq", "depth", None, None),
        check_vma=False,
    )
```

profile of v0, /device:TPU:28, one launch (start us, length us, event | category | flops | bytes accessed | tf_op | source)
XLA Modules:
  0.0 38.1 jit_solution(16438306750472754735)
XLA Ops:
  0.7 35.7 %shard_map.55 = f32[32,1,8,256]{3,2,1,0:T(8,128)} custom-call(f32[1,2,256,256]{3,2,1,0:T(8,128)} %source.1, f32[1,2,256,256]{3,2,1,0:T(8,128)} %receiver.1, s32[1,256,256]{2,1,0:T(8,128)} %classes.1, f32[8,6,2,16]{3,2,1,0:T(2,128)} %bitcast.1, s32[1]{0:T(128)S(6)} %copy.6.freq_row), custom_call_target="tpu_custom_call" | custom-call | tf_op jit(solution)/shard_map/pallas_call | solution.py:411
  36.4 1.7 %broadcast_multiply_fusion = f32[32,1,8,256]{3,2,1,0:T(8,128)} fusion(f32[32,1,8,256]{3,2,1,0:T(8,128)} %shard_map.55), kind=kLoop, calls=%fused_computation | loop fusion | flops 65536 | bytes 524288 | tf_op jit(solution)/shard_map/mul | solution.py:443
where the time goes:
time: 38.3 us; the launch traced here: 38.1 us
  Pallas kernels  35.7 us (93%)
  other arithmetic  1.68 us (4%)
  between operations  0.66 us (2%)
    pallas_call x1, Pallas kernels, per_device(): pl.pallas_call(functools.partial(kernel, cfg), out_shape=jax.ShapeDtypeSt...  35.7 us
    mul x1, other arithmetic, per_device(): return summed * float(nf) ** (-0.5)  1.68 us

commit v1 on v0

--- a/solution.py
+++ b/solution.py
@@ -135,7 +135,7 @@
 
     cls_rows = pl.multiple_of(core * cls_half, SUB)
     cls_copies = []
-    for s in range(1, nd):
+    for s in range(nd - 1, 0, -1):
         to = lax.rem(d + s, nd)
         src_row = pl.multiple_of(window(to) + cls_rows, SUB)
         copy = remote(
@@ -146,8 +146,13 @@
             to,
             f,
         )
-        copy.start()
         cls_copies.append(copy)
+
+    @pl.when(d == 0)
+    def _():
+        for copy in cls_copies:
+            copy.start()
+
 
     def forward(l):
         part = cls.at[l, pl.ds(cls_rows, cls_half)]
@@ -328,6 +333,11 @@
         for k in range(1, K):
             chebyshev(k)
 
+        @pl.when(jnp.logical_and(l == 0, d > 0))
+        def _():
+            for copy in cls_copies:
+                copy.start()
+
         @pl.when(l == 0)
         def _():
             pass_on(0)
@@ -353,9 +363,9 @@
         return carry
 
     lax.fori_loop(0, nd, level, 0)
+    pair_sum(nd - 1)
     if nd >= 2:
         ring_sum(nd - 2)
-    pair_sum(nd - 1)
     ring_sum(nd - 1)
 
     for copy in cls_copies:
@@ -410,7 +420,7 @@
         field = pltpu.VMEM((4, nh, W + 2 * SUB, LANES), jnp.float32)
         summed = pl.pallas_call(
             functools.partial(kernel, cfg),
-            out_shape=jax.ShapeDtypeStruct((rows_out, 1, H, cols_y), jnp.float32),
+            out_shape=pltpu.VMEM((rows_out, 1, H, cols_y), jnp.float32),
             in_specs=[hbm, hbm, hbm, vmem, pl.BlockSpec(memory_space=pltpu.SMEM)],
             out_specs=vmem,
             scratch_shapes=[

time: 38.3 us -> 36.2 us (0.945)
  the two profiles are of different devices: /device:TPU:28 before, /device:TPU:29 now
where the time goes in v1:
time: 36.2 us; the launch traced here: 36 us
  Pallas kernels  34.6 us (96%)
  other arithmetic  0.73 us (2%)
  between operations  0.66 us (2%)
    pallas_call x1, Pallas kernels, per_device(): pl.pallas_call(functools.partial(kernel, cfg), out_shape=pltpu.VMEM((rows...  34.6 us
    mul x1, other arithmetic, per_device(): return summed * float(nf) ** (-0.5)  0.73 us

profile of v1, /device:TPU:29, one launch (start us, length us, event | category | flops | bytes accessed | tf_op | source)
XLA Modules:
  0.0 36.0 jit_solution(772485839382177721)
XLA Ops:
  0.7 34.6 %shard_map.55 = f32[32,1,8,256]{3,2,1,0:T(8,128)S(1)} custom-call(f32[1,2,256,256]{3,2,1,0:T(8,128)} %source.1, f32[1,2,256,256]{3,2,1,0:T(8,128)} %receiver.1, s32[1,256,256]{2,1,0:T(8,128)} %classes.1, f32[8,6,2,16]{3,2,1,0:T(2,128)} %bitcast.1, s32[1]{0:T(128)S(6)} %copy.6.freq_row), custom_call_target="tpu_custom_call" | custom-call | tf_op jit(solution)/shard_map/pallas_call | solution.py:421
  35.3 0.7 %broadcast_multiply_fusion = f32[32,1,8,256]{3,2,1,0:T(8,128)} fusion(f32[32,1,8,256]{3,2,1,0:T(8,128)S(1)} %shard_map.55), kind=kLoop, calls=%fused_computation | loop fusion | flops 65536 | bytes 524288 | tf_op jit(solution)/shard_map/mul | solution.py:453

commit v2 on v1

--- a/solution.py
+++ b/solution.py
@@ -330,21 +330,25 @@
             out_copy(l).start()
 
     def level(l, carry):
-        for k in range(1, K):
+        early = min(3, K)
+        for k in range(1, early):
             chebyshev(k)
+
+        @pl.when(l > 0)
+        def _():
+            pair_sum(l - 1)
 
         @pl.when(jnp.logical_and(l == 0, d > 0))
         def _():
             for copy in cls_copies:
                 copy.start()
 
+        for k in range(early, K):
+            chebyshev(k)
+
         @pl.when(l == 0)
         def _():
             pass_on(0)
-
-        @pl.when(l > 0)
-        def _():
-            pair_sum(l - 1)
 
         classes_ready(l)
         combine(l)

time: 36.2 us -> 35.8 us (0.989)
  the two profiles are of different devices: /device:TPU:29 before, /device:TPU:26 now
where the time goes in v2:
time: 35.8 us; the launch traced here: 35.7 us
  Pallas kernels  34.3 us (96%)
  other arithmetic  0.73 us (2%)
  between operations  0.66 us (2%)
    pallas_call x1, Pallas kernels, per_device(): pl.pallas_call(functools.partial(kernel, cfg), out_shape=pltpu.VMEM((rows...  34.3 us
    mul x1, other arithmetic, per_device(): return summed * float(nf) ** (-0.5)  0.73 us

profile of v2, /device:TPU:26, one launch (start us, length us, event | category | flops | bytes accessed | tf_op | source)
XLA Modules:
  0.0 35.7 jit_solution(1148972112982942421)
XLA Ops:
  0.7 34.3 %shard_map.55 = f32[32,1,8,256]{3,2,1,0:T(8,128)S(1)} custom-call(f32[1,2,256,256]{3,2,1,0:T(8,128)} %source.1, f32[1,2,256,256]{3,2,1,0:T(8,128)} %receiver.1, s32[1,256,256]{2,1,0:T(8,128)} %classes.1, f32[8,6,2,16]{3,2,1,0:T(2,128)} %bitcast.1, s32[1]{0:T(128)S(6)} %copy.6.freq_row), custom_call_target="tpu_custom_call" | custom-call | tf_op jit(solution)/shard_map/pallas_call | solution.py:425
  34.9 0.7 %broadcast_multiply_fusion = f32[32,1,8,256]{3,2,1,0:T(8,128)} fusion(f32[32,1,8,256]{3,2,1,0:T(8,128)S(1)} %shard_map.55), kind=kLoop, calls=%fused_computation | loop fusion | flops 65536 | bytes 524288 | tf_op jit(solution)/shard_map/mul | solution.py:457

commit v3 on v2

--- a/solution.py
+++ b/solution.py
@@ -256,7 +256,7 @@
                     )
 
     def correlate(l, first):
-        group = min(16, half)
+        group = min(32, half)
 
         def step(i, carry):
             for g in range(group):

time: 35.8 us -> 35.8 us (level)
  no operation moved by 1% of the time
where the time goes in v3:
time: 35.8 us; the launch traced here: 35.6 us
  Pallas kernels  34.2 us (96%)
  other arithmetic  0.73 us (2%)
  between operations  0.66 us (2%)
    pallas_call x1, Pallas kernels, per_device(): pl.pallas_call(functools.partial(kernel, cfg), out_shape=pltpu.VMEM((rows...  34.2 us
    mul x1, other arithmetic, per_device(): return summed * float(nf) ** (-0.5)  0.73 us

profile of v3, /device:TPU:26, one launch (start us, length us, event | category | flops | bytes accessed | tf_op | source)
XLA Modules:
  0.0 35.6 jit_solution(11637616808277055663)
XLA Ops:
  0.7 34.2 %shard_map.55 = f32[32,1,8,256]{3,2,1,0:T(8,128)S(1)} custom-call(f32[1,2,256,256]{3,2,1,0:T(8,128)} %source.1, f32[1,2,256,256]{3,2,1,0:T(8,128)} %receiver.1, s32[1,256,256]{2,1,0:T(8,128)} %classes.1, f32[8,6,2,16]{3,2,1,0:T(2,128)} %bitcast.1, s32[1]{0:T(128)S(6)} %copy.6.freq_row), custom_call_target="tpu_custom_call" | custom-call | tf_op jit(solution)/shard_map/pallas_call | solution.py:425
  34.9 0.7 %broadcast_multiply_fusion = f32[32,1,8,256]{3,2,1,0:T(8,128)} fusion(f32[32,1,8,256]{3,2,1,0:T(8,128)S(1)} %shard_map.55), kind=kLoop, calls=%fused_computation | loop fusion | flops 65536 | bytes 524288 | tf_op jit(solution)/shard_map/mul | solution.py:457
